TPU v7x, 32 devices: a whole 2x2x4 slice. The times are simulated.
32 devices in a mesh: slab: 8 (over z, y), brick: 4 (over x, core).
Axes of the slice: x: 2, y: 2, z: 4, core: 2. Of those that a mesh axis runs over, the one named last changes fastest.
Arguments:
- opening_warmth_values: float32 [16, 128, 512], P('slab', 'brick'), may hold values from -6 to 6
- thermal_diffusivity_field: float32 [16, 128, 512], P('slab', 'brick'), may hold values from 0.3 to 3
- atom_released_joules: float32 [8, 4, 8, 128], P('slab', 'brick'), may hold values from 0.1 to 1
- atom_local_coordinates: float32 [8, 4, 8, 3, 128], P('slab', 'brick'), may hold values from 0 to 1
- atom_anchor_voxel: int32 [8, 4, 8, 128], P('slab', 'brick'), may hold values from 0 to 15870, as said below
- atom_oxygen_flag: int32 [8, 4, 8, 128], P('slab', 'brick'), may hold values 0 or 1
- live_entries_number: int32 [8, 4, 8], P('slab', 'brick'), may hold values from 42 to 128, as said below
Outputs:
- advanced_warmth_values: float32 [16, 128, 512], P('slab', 'brick')
- probe_warmth_readout: float32 [8, 4, 8, 128], P('slab', 'brick')
Inputs may be any that keep to these rules, and one draw needn't show every extreme that they name: `atom_anchor_voxel`: each slot's base cell has plane below 1, row below 31 and column below 511 of the owner's block, so all eight corners lie in that block. `live_entries_number`: for every brick index one owner slab receives 128 live slots from every source device; any slot count may be reached elsewhere within the range.
All inputs are finite; a program needn't handle non-finite values. No bound on the sum of `atom_oxygen_flag` on one device may be relied on, other than what follows from the above.
Results may differ from a plain program's by a relative error of at most 0.0003.
Values sent between devices are 32-bit elements; how exact they have to be, the bound alone decides.
A program may use at most 64 MiB of HBM per device.

v0:
```python
import jax
import jax.numpy as jnp
from jax import lax
from jax.sharding import PartitionSpec as P

ITERS = 8


recombine_gain = 3.0
half_interval = 16.0
interval_length = 32.0


def with_halo(block, sides, width):
    for axis, dim in sides:
        count = lax.axis_size(axis)
        forward = [(i, i + 1) for i in range(count - 1)]
        backward = [(target, source) for source, target in forward]
        low = lax.ppermute(
            lax.slice_in_dim(block, block.shape[dim] - width, None, axis=dim), axis, forward
        )
        high = lax.ppermute(lax.slice_in_dim(block, 0, width, axis=dim), axis, backward)
        block = jnp.concatenate([low, block, high], axis=dim)
    return block


def adjacent_sites_list(padded):
    return [
        padded[:-2, 1:-1, 1:-1],
        padded[2:, 1:-1, 1:-1],
        padded[1:-1, :-2, 1:-1],
        padded[1:-1, 2:, 1:-1],
        padded[1:-1, 1:-1, :-2],
        padded[1:-1, 1:-1, 2:],
    ]


def corner_list(frac_z, frac_x, frac_y):
    result = []
    for step_z in (0, 1):
        weight_z = frac_z if step_z else 1.0 - frac_z
        for step_x in (0, 1):
            weight_x = frac_x if step_x else 1.0 - frac_x
            for step_y in (0, 1):
                weight_y = frac_y if step_y else 1.0 - frac_y
                result.append((step_z, step_x, step_y, weight_z * weight_x * weight_y))
    return result


def pad_columns(padded):
    return jnp.pad(padded, ((0, 0), (0, 0), (1, 1)))


def diffusion_matrix(field, coupling_coefficient, main_entry_accumulated):
    padded = with_halo(field, (("slab", 0), ("brick", 1)), 1)
    others = adjacent_sites_list(pad_columns(padded))
    coupled = coupling_coefficient[0] * others[0]
    for index in range(1, 6):
        coupled = coupled + coupling_coefficient[index] * others[index]
    return main_entry_accumulated * field - coupled


def global_sum(first, second):
    return lax.psum(jnp.sum(first * second), ("slab", "brick"))


def per_device(
    opening_warmth_values,
    thermal_diffusivity_field,
    atom_released_joules,
    atom_local_coordinates,
    atom_anchor_voxel,
    atom_oxygen_flag,
    live_entries_number,
):
    layer_number, widened_breadth, domain_length = opening_warmth_values.shape
    plane = widened_breadth * domain_length
    live = (
        lax.broadcasted_iota(jnp.int32, atom_released_joules.shape, 3)
        < live_entries_number[..., None]
    )
    heat = jnp.where(
        live,
        atom_released_joules * (1.0 + recombine_gain * atom_oxygen_flag.astype(jnp.float32)),
        0.0,
    )
    payload = jnp.concatenate([heat[:, :, :, None, :], atom_local_coordinates], axis=3)
    arrived, arrived_cell = (
        lax.all_to_all(payload, "slab", split_axis=2, concat_axis=0, tiled=True),
        lax.all_to_all(
            atom_anchor_voxel[:, :, :, None, :], "slab", split_axis=2, concat_axis=0, tiled=True
        ),
    )
    heat_in = arrived[:, 0, 0, 0, :]
    cells_in = arrived_cell[:, 0, 0, 0, :]
    corners = corner_list(arrived[:, 0, 0, 1, :], arrived[:, 0, 0, 2, :], arrived[:, 0, 0, 3, :])
    targets = []
    amounts = []
    for step_z, step_x, step_y, weight in corners:
        targets.append(cells_in + (step_z * plane + step_x * domain_length + step_y))
        amounts.append(heat_in * weight)
    flat_source = jnp.zeros((layer_number * plane,), jnp.float32)
    flat_source = flat_source.at[jnp.concatenate([item.reshape(-1) for item in targets])].add(
        jnp.concatenate([item.reshape(-1) for item in amounts])
    )
    deposited_power = flat_source.reshape(layer_number, widened_breadth, domain_length)
    kpadded = with_halo(thermal_diffusivity_field, (("slab", 0), ("brick", 1)), 1)
    coupling_coefficient = [
        0.5 * (thermal_diffusivity_field + other)
        for other in adjacent_sites_list(pad_columns(kpadded))
    ]
    main_entry_accumulated = coupling_coefficient[0]
    for index in range(1, 6):
        main_entry_accumulated = main_entry_accumulated + coupling_coefficient[index]
    starting_contribution = diffusion_matrix(
        opening_warmth_values, coupling_coefficient, main_entry_accumulated
    )
    linear_system_load = (
        opening_warmth_values
        - half_interval * starting_contribution
        + interval_length * deposited_power
    )
    advanced_warmth_values = opening_warmth_values
    equation_mismatch = linear_system_load - (
        opening_warmth_values + half_interval * starting_contribution
    )
    compass_heading = equation_mismatch
    norm_now = global_sum(equation_mismatch, equation_mismatch)
    for step in range(ITERS):
        image = compass_heading + half_interval * diffusion_matrix(
            compass_heading, coupling_coefficient, main_entry_accumulated
        )
        implicit_blend = norm_now / lax.psum(jnp.sum(compass_heading * image), ("slab", "brick"))
        advanced_warmth_values = advanced_warmth_values + implicit_blend * compass_heading
        equation_mismatch = equation_mismatch - implicit_blend * image
        norm_next = global_sum(equation_mismatch, equation_mismatch)
        compass_heading = equation_mismatch + norm_next / norm_now * compass_heading
        norm_now = norm_next
    raveled_fresh = advanced_warmth_values.reshape(-1)
    gathered = jnp.zeros(heat_in.shape, jnp.float32)
    for index in range(8):
        gathered = gathered + corners[index][3] * raveled_fresh[targets[index]]
    injected_warmth_rates = gathered.shape[0]
    returned = lax.all_to_all(
        gathered.reshape(injected_warmth_rates, 1, 1, gathered.shape[1]),
        "slab",
        split_axis=0,
        concat_axis=2,
        tiled=True,
    )
    probe_warmth_readout = jnp.where(live, returned, 0.0)
    return (advanced_warmth_values, probe_warmth_readout)


def solution(mesh):
    placed = (
        P("slab", "brick", None),
        P("slab", "brick", None),
        P("slab", "brick", None, None),
        P("slab", "brick", None, None, None),
        P("slab", "brick", None, None),
        P("slab", "brick", None, None),
        P("slab", "brick", None),
    )
    return jax.shard_map(
        per_device,
        mesh=mesh,
        in_specs=placed,
        out_specs=(P("slab", "brick", None), P("slab", "brick", None, None)),
        check_vma=False,
    )
```

profile of v0, /device:TPU:0, one launch (start us, length us, event | category | flops | bytes accessed | tf_op | source)
XLA Modules:
  0.0 925.8 jit_solution(3003184932355336233)
XLA Ops:
  0.6 7.3 all-to-all-start
  21.4 7.5 all-to-all-start.1
  29.1 6.4 all-to-all-done.1
  35.6 43.2 %scatter_custom_fusion = f32[32768]{0:T(1024)S(1)} fusion(s32[8192]{0:T(1024)S(1)} %bitcast.161, f32[8192]{0:T(1024)S(1)} %constant_dynamic-update-slice_fusion.15, f32[]{:T(128)} %constant.9.clone.1), kind=kCustom, calls=%fused_computation.292 | custom fusion | flops 8192 | bytes 131076 | tf_op jit(solution)/shard_map/scatter-add | solution.py:103
  108.7 41.3 %all-reduce.10 = (f32[]{:T(128)}, f32[]{:T(128)}) all-reduce(f32[]{:T(128)} %get-tuple-element.3, f32[]{:T(128)} %get-tuple-element.2), channel_id=1, replica_groups=mesh['slab'=8,'brick'=4] {'slab','brick'}, use_global_device_ids=true, to_apply=%region_2.3 | all-reduce | flops 2 | bytes 16 | tf_op jit(solution)/shard_map/psum | solution.py:64
  151.9 39.8 %psum.114 = f32[]{:T(128)} all-reduce(f32[]{:T(128)} %multiply_reduce_fusion.12), channel_id=1, replica_groups=mesh['slab'=8,'brick'=4] {'slab','brick'}, use_global_device_ids=true, to_apply=%region_6.7 | all-reduce | flops 1 | bytes 8 | tf_op jit(solution)/shard_map/psum | solution.py:64
  211.3 39.8 %psum.115 = f32[]{:T(128)} all-reduce(f32[]{:T(128)} %get-tuple-element.26), channel_id=1, replica_groups=mesh['slab'=8,'brick'=4] {'slab','brick'}, use_global_device_ids=true, to_apply=%region_8.9 | all-reduce | flops 1 | bytes 8 | tf_op jit(solution)/shard_map/psum | solution.py:133
  253.0 40.9 %psum.116 = f32[]{:T(128)} all-reduce(f32[]{:T(128)} %get-tuple-element.24), channel_id=1, replica_groups=mesh['slab'=8,'brick'=4] {'slab','brick'}, use_global_device_ids=true, to_apply=%region_10.11 | all-reduce | flops 1 | bytes 8 | tf_op jit(solution)/shard_map/psum | solution.py:64
  312.4 40.8 %psum.117 = f32[]{:T(128)} all-reduce(f32[]{:T(128)} %get-tuple-element.22), channel_id=1, replica_groups=mesh['slab'=8,'brick'=4] {'slab','brick'}, use_global_device_ids=true, to_apply=%region_12.13 | all-reduce | flops 1 | bytes 8 | tf_op jit(solution)/shard_map/psum | solution.py:133
  355.2 39.9 %psum.118 = f32[]{:T(128)} all-reduce(f32[]{:T(128)} %get-tuple-element.20), channel_id=1, replica_groups=mesh['slab'=8,'brick'=4] {'slab','brick'}, use_global_device_ids=true, to_apply=%region_14.15 | all-reduce | flops 1 | bytes 8 | tf_op jit(solution)/shard_map/psum | solution.py:64
  414.4 40.6 %psum.119 = f32[]{:T(128)} all-reduce(f32[]{:T(128)} %get-tuple-element.18), channel_id=1, replica_groups=mesh['slab'=8,'brick'=4] {'slab','brick'}, use_global_device_ids=true, to_apply=%region_16.17 | all-reduce | flops 1 | bytes 8 | tf_op jit(solution)/shard_map/psum | solution.py:133
  457.0 40.1 %psum.120 = f32[]{:T(128)} all-reduce(f32[]{:T(128)} %get-tuple-element.16), channel_id=1, replica_groups=mesh['slab'=8,'brick'=4] {'slab','brick'}, use_global_device_ids=true, to_apply=%region_18.19 | all-reduce | flops 1 | bytes 8 | tf_op jit(solution)/shard_map/psum | solution.py:64
  515.7 41.7 %psum.121 = f32[]{:T(128)} all-reduce(f32[]{:T(128)} %get-tuple-element.14), channel_id=1, replica_groups=mesh['slab'=8,'brick'=4] {'slab','brick'}, use_global_device_ids=true, to_apply=%region_20.21 | all-reduce | flops 1 | bytes 8 | tf_op jit(solution)/shard_map/psum | solution.py:133
  559.4 39.1 %psum.122 = f32[]{:T(128)} all-reduce(f32[]{:T(128)} %get-tuple-element.12), channel_id=1, replica_groups=mesh['slab'=8,'brick'=4] {'slab','brick'}, use_global_device_ids=true, to_apply=%region_22.23 | all-reduce | flops 1 | bytes 8 | tf_op jit(solution)/shard_map/psum | solution.py:64
  618.0 40.7 %psum.123 = f32[]{:T(128)} all-reduce(f32[]{:T(128)} %get-tuple-element.10), channel_id=1, replica_groups=mesh['slab'=8,'brick'=4] {'slab','brick'}, use_global_device_ids=true, to_apply=%region_24.25 | all-reduce | flops 1 | bytes 8 | tf_op jit(solution)/shard_map/psum | solution.py:133
  660.6 40.0 %psum.124 = f32[]{:T(128)} all-reduce(f32[]{:T(128)} %get-tuple-element.8), channel_id=1, replica_groups=mesh['slab'=8,'brick'=4] {'slab','brick'}, use_global_device_ids=true, to_apply=%region_26.27 | all-reduce | flops 1 | bytes 8 | tf_op jit(solution)/shard_map/psum | solution.py:64
  719.9 40.7 %psum.125 = f32[]{:T(128)} all-reduce(f32[]{:T(128)} %get-tuple-element.6), channel_id=1, replica_groups=mesh['slab'=8,'brick'=4] {'slab','brick'}, use_global_device_ids=true, to_apply=%region_28.29 | all-reduce | flops 1 | bytes 8 | tf_op jit(solution)/shard_map/psum | solution.py:133
  762.6 40.0 %psum.126 = f32[]{:T(128)} all-reduce(f32[]{:T(128)} %multiply_reduce_fusion), channel_id=1, replica_groups=mesh['slab'=8,'brick'=4] {'slab','brick'}, use_global_device_ids=true, to_apply=%region_30.31 | all-reduce | flops 1 | bytes 8 | tf_op jit(solution)/shard_map/psum | solution.py:64
  822.0 40.0 %psum.127 = f32[]{:T(128)} all-reduce(f32[]{:T(128)} %fusion.1), channel_id=1, replica_groups=mesh['slab'=8,'brick'=4] {'slab','brick'}, use_global_device_ids=true, to_apply=%region_32.33 | all-reduce | flops 1 | bytes 8 | tf_op jit(solution)/shard_map/psum | solution.py:133
  870.3 6.2 gather_fusion.1
  876.4 6.2 gather_fusion.2
  882.6 6.2 gather_fusion.3
  888.7 6.2 gather_fusion.4
  913.4 11.7 %all_to_all.33 = f32[8,1,1,128]{3,2,1,0:T(1,128)S(1)} all-to-all(f32[8,1,1,128]{3,2,1,0:T(1,128)S(1)} %bitcast.163), channel_id=1, replica_groups=mesh['slab'=8,'brick'=4] {'slab'}, dimensions={0} | all-to-all | bytes 8192 | tf_op jit(solution)/shard_map/all_to_all | solution.py:144
  (186 shorter events, 197.8 us)
Async XLA Ops:
  0.6 20.8 %all-to-all-start = ((s32[1,1,8,1,128]{4,3,1,0,2:T(1,128)}), s32[1,1,8,1,128]{4,3,1,0,2:T(1,128)S(1)}, u32[]{:S(2)}, u32[]{:S(2)}) async-start(s32[1,1,8,1,128]{4,3,1,0,2:T(1,128)} %bitcast.165), calls=%async_computation | async-start | bytes 8192 | tf_op jit(solution)/shard_map/all_to_all | solution.py:90
  8.8 70.1 %collective-permute-start = (f32[1,32,512]{2,1,0:T(8,128)S(1)}, f32[1,32,512]{2,1,0:T(8,128)S(1)}, u32[]{:S(2)}, u32[]{:S(2)}) collective-permute-start(f32[1,32,512]{2,1,0:T(8,128)S(1)} %get-tuple-element.73), channel_id=1, source_target_pairs={{0,4},{4,8},{8,12},{12,16},{16,20},{20,24},{24,28},{1,5},{5,9},{9,... | collective-permute-start | bytes 196616 | tf_op jit(solution)/shard_map/ppermute | solution.py:19
  12.8 67.0 %collective-permute-start.1 = (f32[1,32,512]{2,1,0:T(8,128)S(1)}, f32[1,32,512]{2,1,0:T(8,128)S(1)}, u32[]{:S(2)}, u32[]{:S(2)}) collective-permute-start(f32[1,32,512]{2,1,0:T(8,128)S(1)} %get-tuple-element.72), channel_id=1, source_target_pairs={{4,0},{8,4},{12,8},{16,12},{20,16},{24,20},{28,24},{5,1},{9,5},{13... | collective-permute-start | bytes 196616 | tf_op jit(solution)/shard_map/ppermute | solution.py:22
  14.1 68.3 %collective-permute-start.4 = (f32[1,32,512]{2,1,0:T(8,128)S(1)}, f32[1,32,512]{2,1,0:T(8,128)S(1)}, u32[]{:S(2)}, u32[]{:S(2)}) collective-permute-start(f32[1,32,512]{2,1,0:T(8,128)S(1)} %get-tuple-element.75), channel_id=1, source_target_pairs={{0,4},{4,8},{8,12},{12,16},{16,20},{20,24},{24,28},{1,5},{5,9},{9,... | collective-permute-start | bytes 196616 | tf_op jit(solution)/shard_map/ppermute | solution.py:19
  18.7 63.8 %collective-permute-start.5 = (f32[1,32,512]{2,1,0:T(8,128)S(1)}, f32[1,32,512]{2,1,0:T(8,128)S(1)}, u32[]{:S(2)}, u32[]{:S(2)}) collective-permute-start(f32[1,32,512]{2,1,0:T(8,128)S(1)} %get-tuple-element.74), channel_id=1, source_target_pairs={{4,0},{8,4},{12,8},{16,12},{20,16},{24,20},{28,24},{5,1},{9,5},{13... | collective-permute-start | bytes 196616 | tf_op jit(solution)/shard_map/ppermute | solution.py:22
  21.4 14.1 %all-to-all-start.1 = ((f32[1,1,8,4,128]{4,3,1,0,2:T(4,128)}), f32[1,1,8,4,128]{4,3,1,0,2:T(4,128)S(1)}, u32[]{:S(2)}, u32[]{:S(2)}) async-start(f32[1,1,8,4,128]{4,3,1,0,2:T(4,128)} %pad_maximum_fusion.72), calls=%async_computation.1 | async-start | bytes 32768 | tf_op jit(solution)/shard_map/all_to_all | solution.py:89
  79.9 8.8 collective-permute-start.2
  81.2 7.5 collective-permute-start.3
  82.6 6.3 collective-permute-start.6
  94.6 6.2 collective-permute-start.9
  193.2 6.3 collective-permute-start.12
  197.6 6.2 collective-permute-start.13
  295.3 6.9 collective-permute-start.16
  299.7 6.2 collective-permute-start.17
  396.5 6.3 collective-permute-start.20
  400.8 6.2 collective-permute-start.21
  498.5 6.4 collective-permute-start.24
  503.0 6.2 collective-permute-start.25
  599.9 6.3 collective-permute-start.28
  604.3 6.2 collective-permute-start.29
  702.0 6.3 collective-permute-start.32
  706.4 6.2 collective-permute-start.33
  804.0 6.3 collective-permute-start.36
  808.4 6.2 collective-permute-start.37
  (25 other events, 84.9 us)
where the time goes:
time: 930 us; the launch traced here: 926 us
  blocking collectives  617 us (66%)
  starting transfers between devices  100 us (11%)
  waiting for transfers between devices  75.8 us (8%)
  other arithmetic  58.3 us (6%)
  local copies, waits for them, and re-layouts  52.5 us (6%)
  between operations  21.7 us (2%)
    psum x8, blocking collectives, global_sum(): return lax.psum(jnp.sum(first * second), ('slab', 'brick'))  321 us
    psum x7, blocking collectives, per_device(): lax.psum(jnp.sum(compass_heading * image), ('slab', 'brick'))  284 us
    ppermute x20, waiting for transfers between devices, with_halo(): lax.ppermute(lax.slice_in_dim(block, 0, width, axis=dim), axis, backward)  64 us
    ppermute x20, starting transfers between devices, with_halo(): lax.ppermute(lax.slice_in_dim(block, block.shape[dim] - width, None, axis...  59.6 us
    gather x8, local copies, waits for them, and re-layouts, per_device(): gathered = gathered + corners[index][3] * raveled_fresh[targets[index]]  49.2 us
    scatter-add x1, other arithmetic, per_device(): flat_source.at[jnp.concatenate([item.reshape(-1) for item in targets])]  43.2 us
    ppermute x20, starting transfers between devices, with_halo(): lax.ppermute(lax.slice_in_dim(block, 0, width, axis=dim), axis, backward)  25.8 us
  transfers between devices with their start and end apart: 42, of which 26 were waited for; matrix products, arithmetic and copies ran while one was open for 5% of the time, Pallas kernels for 0%

commit v1 on v0

v1 whole, which is shorter than its diff:
```python
import functools

import jax
import jax.numpy as jnp
from jax import lax
from jax.experimental import pallas as pl
from jax.experimental.pallas import tpu as pltpu
from jax.sharding import PartitionSpec as P

ITERS = 8
recombine_gain = 3.0
half_interval = 16.0
interval_length = 32.0
MESH_ID = pl.DeviceIdType.MESH
HIGHEST = lax.Precision.HIGHEST
ROUNDS = ITERS + 2


def step_kernel(
    ns,
    nb,
    layers,
    chunk,
    v_ref,
    k_ref,
    joules_ref,
    local_ref,
    anchor_ref,
    oxygen_ref,
    entries_ref,
    x_ref,
    probe_ref,
    coef,
    fields,
    vectors,
    halo_z,
    halo_x,
    face_x,
    sums,
    atoms_out,
    atoms_in,
    weight_zx,
    weight_y,
    read_out,
    read_in,
    halo_send,
    halo_recv,
    sum_send,
    sum_recv,
    atom_send,
    atom_recv,
    read_send,
    read_recv,
):
    s = lax.axis_index("slab")
    b = lax.axis_index("brick")
    rows, columns = v_ref.shape
    lines = rows // layers
    slots = joules_ref.shape[1]
    devices = ns * nb
    me = s * nb + b

    def wrapped(index, count):
        return jnp.where(index >= count, index - count, index)

    def for_peers(action):
        for shift in range(1, nb):
            action(s, wrapped(b + shift, nb))

        def outer(step, carry):
            for shift in range(nb):
                action(wrapped(s + step, ns), wrapped(b + shift, nb))
            return carry

        lax.fori_loop(1, ns, outer, 0)

    barrier = pltpu.get_barrier_semaphore()
    for_peers(
        lambda ps, pb: pl.semaphore_signal(
            barrier, inc=1, device_id=(ps, pb), device_id_type=MESH_ID
        )
    )

    low_slab, high_slab = s > 0, s < ns - 1
    low_brick, high_brick = b > 0, b < nb - 1

    @pl.when(s == 0)
    def _():
        halo_z[:, 0] = jnp.zeros_like(halo_z[:, 0])

    @pl.when(s == ns - 1)
    def _():
        halo_z[:, 1] = jnp.zeros_like(halo_z[:, 1])

    @pl.when(b == 0)
    def _():
        halo_x[:, 0] = jnp.zeros_like(halo_x[:, 0])

    @pl.when(b == nb - 1)
    def _():
        halo_x[:, 1] = jnp.zeros_like(halo_x[:, 1])

    def halo_parts(turn, block):
        top = pl.ds(rows - lines, lines)
        return (
            (high_slab, low_slab, block.at[top], halo_z.at[turn, 0], (s + 1, b)),
            (low_slab, high_slab, block.at[pl.ds(0, lines)], halo_z.at[turn, 1], (s - 1, b)),
            (high_brick, low_brick, face_x.at[turn, 0], halo_x.at[turn, 0], (s, b + 1)),
            (low_brick, high_brick, face_x.at[turn, 1], halo_x.at[turn, 1], (s, b - 1)),
        )

    def halo_copy(turn, way, source, target, device):
        return pltpu.make_async_remote_copy(
            src_ref=source,
            dst_ref=target,
            send_sem=halo_send.at[turn, way],
            recv_sem=halo_recv.at[turn, way],
            device_id=device,
            device_id_type=MESH_ID,
        )

    def stage_faces(turn, block):
        for z in range(layers):
            first, last = z * lines, z * lines + lines - 1
            face_x[turn, 0, pl.ds(z, 1), :] = block[pl.ds(last, 1), :]
            face_x[turn, 1, pl.ds(z, 1), :] = block[pl.ds(first, 1), :]

    def start_halo(turn, block):
        for way, (sends, _, source, target, device) in enumerate(halo_parts(turn, block)):

            @pl.when(sends)
            def _():
                halo_copy(turn, way, source, target, device).start()

    def wait_halo(turn, block):
        for way, (_, receives, source, target, device) in enumerate(halo_parts(turn, block)):

            @pl.when(receives)
            def _():
                halo_copy(turn, way, source, target, device).wait_recv()

    def end_halo(turn, block):
        for way, (sends, _, source, target, device) in enumerate(halo_parts(turn, block)):

            @pl.when(sends)
            def _():
                halo_copy(turn, way, source, target, device).wait_send()

    def atom_copy(peer, source, target, out_sem, in_sem):
        return pltpu.make_async_remote_copy(
            src_ref=source,
            dst_ref=target,
            send_sem=out_sem,
            recv_sem=in_sem,
            device_id=(peer, b),
            device_id_type=MESH_ID,
        )

    def for_slabs(action):
        def body(step, carry):
            action(wrapped(s + step, ns))
            return carry

        lax.fori_loop(1, ns, body, 0)

    row_of = lax.broadcasted_iota(jnp.int32, (ns, slots), 0)
    limit = jnp.zeros((ns, slots), jnp.int32)
    for owner in range(ns):
        limit = jnp.where(row_of == owner, entries_ref[owner], limit)
    live = lax.broadcasted_iota(jnp.int32, (ns, slots), 1) < limit
    heat = jnp.where(
        live,
        joules_ref[...] * (1.0 + recombine_gain * oxygen_ref[...].astype(jnp.float32)),
        0.0,
    )
    anchor = anchor_ref[...]
    line = anchor // columns
    column = (anchor - line * columns).astype(jnp.float32)
    line = line.astype(jnp.float32)
    for owner in range(ns):
        here = slice(owner, owner + 1)
        atoms_out[owner, 0:1, :] = heat[here]
        atoms_out[owner, 1:4, :] = local_ref[owner]
        atoms_out[owner, 4:5, :] = line[here]
        atoms_out[owner, 5:6, :] = column[here]
        atoms_out[owner, 6:8, :] = jnp.zeros((2, slots), jnp.float32)
    stage_faces(0, k_ref)
    stage_faces(1, v_ref)
    pl.semaphore_wait(barrier, devices - 1)

    for_slabs(
        lambda peer: atom_copy(
            peer, atoms_out.at[peer], atoms_in.at[s], atom_send, atom_recv
        ).start()
    )
    start_halo(0, k_ref)
    start_halo(1, v_ref)
    atoms_in[s] = atoms_out[s]
    others = pl.ds(0, ns - 1)
    atom_copy(
        wrapped(s + 1, ns), atoms_out.at[others], atoms_in.at[others], atom_send, atom_recv
    ).wait()

    line_at = lax.broadcasted_iota(jnp.int32, (rows, slots), 0).astype(jnp.float32)
    column_at = lax.broadcasted_iota(jnp.int32, (columns, slots), 0).astype(jnp.float32)

    def deposit(part, total):
        warmed = []
        for index in range(chunk):
            packed = atoms_in[part * chunk + index]
            fz, fx, fy = packed[1:2], packed[2:3], packed[3:4]
            off = line_at - packed[4:5]
            gz, gx = 1.0 - fz, 1.0 - fx
            plain = jnp.where(off == 0.0, gz * gx, 0.0)
            plain = jnp.where(off == 1.0, gz * fx, plain)
            plain = jnp.where(off == float(lines), fz * gx, plain)
            plain = jnp.where(off == float(lines + 1), fz * fx, plain)
            offy = column_at - packed[5:6]
            lane = pl.ds(index * slots, slots)
            weight_zx[part, :, lane] = plain
            weight_y[part, :, lane] = jnp.where(
                offy == 0.0, 1.0 - fy, jnp.where(offy == 1.0, fy, 0.0)
            )
            warmed.append(plain * packed[0:1])
        return total + lax.dot_general(
            jnp.concatenate(warmed, axis=1),
            weight_y[part],
            (((1,), (1,)), ((), ())),
            precision=HIGHEST,
            preferred_element_type=jnp.float32,
        )

    source = lax.fori_loop(
        0, ns // chunk, deposit, jnp.zeros((rows, columns), jnp.float32)
    )

    row = lax.broadcasted_iota(jnp.int32, (rows, columns), 0)
    col = lax.broadcasted_iota(jnp.int32, (rows, columns), 1)
    within = row % lines
    first_line, last_line = within == 0, within == lines - 1

    def neighbours(block, turn):
        low_z, high_z = halo_z[turn, 0], halo_z[turn, 1]
        below = jnp.concatenate([low_z, block[: rows - lines]], axis=0)
        above = jnp.concatenate([block[lines:], high_z], axis=0)
        low_x = jnp.concatenate(
            [
                jnp.broadcast_to(halo_x[turn, 0, pl.ds(z, 1), :], (lines, columns))
                for z in range(layers)
            ],
            axis=0,
        )
        high_x = jnp.concatenate(
            [
                jnp.broadcast_to(halo_x[turn, 1, pl.ds(z, 1), :], (lines, columns))
                for z in range(layers)
            ],
            axis=0,
        )
        left = jnp.where(first_line, low_x, pltpu.roll(block, 1, 0))
        right = jnp.where(last_line, high_x, pltpu.roll(block, rows - 1, 0))
        before = pltpu.roll(block, 1, 1)
        after = pltpu.roll(block, columns - 1, 1)
        return below, above, left, right, before, after

    def operator(block, turn):
        near = neighbours(block, turn)
        out = coef[6] * block
        for index in range(6):
            out = out - coef[index] * near[index]
        return out

    wait_halo(0, k_ref)
    k = k_ref[...]
    inside = (
        (row >= lines) | low_slab,
        (row < rows - lines) | high_slab,
        jnp.logical_not(first_line) | low_brick,
        jnp.logical_not(last_line) | high_brick,
        col > 0,
        col < columns - 1,
    )
    diagonal = jnp.zeros((rows, columns), jnp.float32)
    for index, other in enumerate(neighbours(k, 0)):
        face = (0.5 * half_interval) * (k + jnp.where(inside[index], other, 0.0))
        coef[index] = jnp.where(inside[index], face, 0.0)
        diagonal = diagonal + face
    coef[6] = 1.0 + diagonal

    wait_halo(1, v_ref)
    v = v_ref[...]
    near = neighbours(v, 1)
    spread = diagonal * v
    for index in range(6):
        spread = spread - coef[index] * near[index]
    residual = interval_length * source - 2.0 * spread
    fields[0] = residual
    stage_faces(2, fields.at[0])
    start_halo(2, fields.at[0])
    vectors[0] = residual
    x_ref[...] = v
    wait_halo(2, fields.at[0])
    fields[1] = operator(residual, 2)

    before_rr = None
    before_alpha = None
    for step in range(ITERS):
        last = step == ITERS - 1
        image = fields.at[step + 1]
        turn = step + 3
        if not last:
            stage_faces(turn, image)
            start_halo(turn, image)
        r = vectors[0]
        w = image[...]
        sums[step, me] = jnp.concatenate(
            [
                functools.reduce(
                    jnp.add,
                    [
                        jnp.sum(item, axis=0, keepdims=True)[:, at : at + 128]
                        for at in range(0, columns, 128)
                    ],
                )
                for item in (r * r, r * w)
            ],
            axis=0,
        )

        def sum_copy(part, ps, pb):
            return pltpu.make_async_remote_copy(
                src_ref=part,
                dst_ref=part,
                send_sem=sum_send.at[step],
                recv_sem=sum_recv.at[step],
                device_id=(ps, pb),
                device_id_type=MESH_ID,
            )

        for_peers(lambda ps, pb: sum_copy(sums.at[step, me], ps, pb).start())
        if not last:
            wait_halo(turn, image)
            q = operator(w, turn)
        sum_copy(
            sums.at[step, pl.ds(0, devices - 1)], wrapped(s + 1, ns), b
        ).wait()
        total = jnp.sum(
            jnp.sum(sums[step], axis=0), axis=1, keepdims=True
        )
        rr, rw = total[0:1], total[1:2]
        if step == 0:
            alpha = rr / rw
            p = r
            sp = w
            zp = q
        else:
            beta = rr / before_rr
            alpha = rr / (rw - beta * rr / before_alpha)
            p = r + beta * vectors[1]
            if not last:
                sp = w + beta * vectors[2]
                zp = q + beta * vectors[3]
        x_ref[...] = x_ref[...] + alpha * p
        if not last:
            vectors[0] = r - alpha * sp
            fields[step + 2] = w - alpha * zp
            vectors[1] = p
            vectors[2] = sp
            vectors[3] = zp
        before_rr, before_alpha = rr, alpha

    x = x_ref[...]

    def interpolate(part, carry):
        lifted = jnp.dot(
            x, weight_y[part], precision=HIGHEST, preferred_element_type=jnp.float32
        )
        read = jnp.sum(lifted * weight_zx[part], axis=0, keepdims=True)
        for index in range(chunk):
            read_out[part * chunk + index] = read[:, index * slots : (index + 1) * slots]
        return carry

    lax.fori_loop(0, ns // chunk, interpolate, 0)
    for_slabs(
        lambda peer: atom_copy(
            peer, read_out.at[peer], read_in.at[s], read_send, read_recv
        ).start()
    )
    read_in[s] = read_out[s]
    end_halo(0, k_ref)
    end_halo(1, v_ref)
    for turn in range(2, ROUNDS):
        end_halo(turn, fields.at[turn - 2])
    atom_copy(
        wrapped(s + 1, ns), read_out.at[others], read_in.at[others], read_send, read_recv
    ).wait()
    for owner in range(ns):
        probe_ref[owner : owner + 1, :] = jnp.where(
            live[owner : owner + 1], read_in[owner], 0.0
        )


def per_device(
    ns,
    nb,
    opening_warmth_values,
    thermal_diffusivity_field,
    atom_released_joules,
    atom_local_coordinates,
    atom_anchor_voxel,
    atom_oxygen_flag,
    live_entries_number,
):
    layers, lines, columns = opening_warmth_values.shape
    slots = atom_released_joules.shape[-1]
    rows = layers * lines
    chunk = 8 if ns % 8 == 0 else ns
    parts = ns // chunk
    f32 = jnp.float32
    vmem = pl.BlockSpec(memory_space=pltpu.VMEM)
    dma = pltpu.SemaphoreType.DMA
    x, probe = pl.pallas_call(
        functools.partial(step_kernel, ns, nb, layers, chunk),
        out_shape=(
            jax.ShapeDtypeStruct((rows, columns), f32),
            jax.ShapeDtypeStruct((ns, slots), f32),
        ),
        in_specs=[vmem] * 6 + [pl.BlockSpec(memory_space=pltpu.SMEM)],
        out_specs=(vmem, vmem),
        scratch_shapes=[
            pltpu.VMEM((7, rows, columns), f32),
            pltpu.VMEM((ITERS + 1, rows, columns), f32),
            pltpu.VMEM((4, rows, columns), f32),
            pltpu.VMEM((ROUNDS, 2, lines, columns), f32),
            pltpu.VMEM((ROUNDS, 2, layers, columns), f32),
            pltpu.VMEM((ROUNDS, 2, layers, columns), f32),
            pltpu.VMEM((ITERS, ns * nb, 2, 128), f32),
            pltpu.VMEM((ns, 8, slots), f32),
            pltpu.VMEM((ns, 8, slots), f32),
            pltpu.VMEM((parts, rows, chunk * slots), f32),
            pltpu.VMEM((parts, columns, chunk * slots), f32),
            pltpu.VMEM((ns, 1, slots), f32),
            pltpu.VMEM((ns, 1, slots), f32),
            dma((ROUNDS, 4)),
            dma((ROUNDS, 4)),
            dma((ITERS,)),
            dma((ITERS,)),
            dma,
            dma,
            dma,
            dma,
        ],
        compiler_params=pltpu.CompilerParams(
            collective_id=0, has_side_effects=True, vmem_limit_bytes=48 * 1024 * 1024
        ),
        name="heat_step",
    )(
        opening_warmth_values.reshape(rows, columns),
        thermal_diffusivity_field.reshape(rows, columns),
        atom_released_joules.reshape(ns, slots),
        atom_local_coordinates.reshape(ns, 3, slots),
        atom_anchor_voxel.reshape(ns, slots),
        atom_oxygen_flag.reshape(ns, slots),
        live_entries_number.reshape(ns),
    )
    return x.reshape(layers, lines, columns), probe.reshape(1, 1, ns, slots)


def solution(mesh):
    placed = (
        P("slab", "brick", None),
        P("slab", "brick", None),
        P("slab", "brick", None, None),
        P("slab", "brick", None, None, None),
        P("slab", "brick", None, None),
        P("slab", "brick", None, None),
        P("slab", "brick", None),
    )
    return jax.shard_map(
        functools.partial(per_device, mesh.shape["slab"], mesh.shape["brick"]),
        mesh=mesh,
        in_specs=placed,
        out_specs=(P("slab", "brick", None), P("slab", "brick", None, None)),
        check_vma=False,
    )
```

time: 930 us -> 75 us (0.08)
  blocking collectives: 617 us -> 0 us
  starting transfers between devices: 100 us -> 0 us
  waiting for transfers between devices: 75.8 us -> 0 us
  Pallas kernels: 0 us -> 69.7 us
  other arithmetic: 58.3 us -> 0 us
  local copies, waits for them, and re-layouts: 52.5 us -> 4.43 us
  between operations: 21.7 us -> 0.69 us
    psum x15 -> x0, blocking collectives: 605 us -> none  [the longest x8 321 us: global_sum(): return lax.psum(jnp.sum(first * second), ('slab', 'brick'))]
    ppermute x40 -> x0, starting transfers between devices: 85.5 us -> none  [the longest x20 59.6 us: with_halo(): lax.ppermute(lax.slice_in_dim(block, block.shape[dim] - width, None, axis...]
    pallas_call x0 -> x1, Pallas kernels: none -> 69.7 us  [per_device(): pl.pallas_call(functools.partial(step_kernel, ns, nb, layers, chunk), out...]
    ppermute x40 -> x0, waiting for transfers between devices: 69.4 us -> none  [the longest x20 64 us: with_halo(): lax.ppermute(lax.slice_in_dim(block, 0, width, axis=dim), axis, backward)]
    gather x8 -> x0, local copies, waits for them, and re-layouts: 49.2 us -> none  [per_device(): gathered = gathered + corners[index][3] * raveled_fresh[targets[index]]]
    scatter-add x1 -> x0, other arithmetic: 43.2 us -> none  [per_device(): flat_source.at[jnp.concatenate([item.reshape(-1) for item in targets])]]
    all_to_all x2 -> x0, starting transfers between devices: 14.8 us -> none  [the longest x1 7.52 us: per_device(): lax.all_to_all(payload, 'slab', split_axis=2, concat_axis=0, tiled=True)]
    all_to_all x1 -> x0, blocking collectives: 11.7 us -> none  [per_device(): lax.all_to_all(gathered.reshape(injected_warmth_rates, 1, 1, gathered.sha...]
  transfers between devices with their start and end apart: 42 -> 0, of which waited for: 26 -> 0; matrix products, arithmetic and copies ran while one was open for 5% -> 0% of each run, Pallas kernels for 0% -> 0%
where the time goes in v1:
time: 75 us; the launch traced here: 74.8 us
  Pallas kernels  69.7 us (93%)
  local copies, waits for them, and re-layouts  4.43 us (6%)
    pallas_call x1, Pallas kernels, per_device(): pl.pallas_call(functools.partial(step_kernel, ns, nb, layers, chunk), out...  69.7 us
    unnamed x15, local copies, waits for them, and re-layouts  4.43 us

profile of v1, /device:TPU:0, one launch (start us, length us, event | category | flops | bytes accessed | tf_op | source)
XLA Modules:
  0.0 74.8 jit_solution(13192054335399897266)
XLA Ops:
  0.6 0.0 copy-start.2
  0.6 0.0 copy-start.3
  0.7 0.0 copy-start.4
  0.7 0.7 copy.11
  1.4 0.0 copy-start.5
  1.4 0.0 copy-done.2
  1.4 0.0 copy-done.3
  1.4 0.0 copy-done.4
  1.4 0.6 copy-done.5
  2.0 0.0 copy-start
  2.0 0.9 %copy-done = f32[2,32,512]{2,1,0:T(8,128)S(1)} copy-done((f32[2,32,512]{2,1,0:T(8,128)S(1)}, f32[2,32,512]{2,1,0:T(8,128)}, u32[]{:S(2)}) %copy-start) | copy-done | bytes 131096
  3.0 0.0 copy-start.1
  3.0 0.9 %copy-done.1 = f32[2,32,512]{2,1,0:T(8,128)S(1)} copy-done((f32[2,32,512]{2,1,0:T(8,128)S(1)}, f32[2,32,512]{2,1,0:T(8,128)}, u32[]{:S(2)}) %copy-start.1) | copy-done | bytes 131096
  3.9 69.7 %heat_step.1 = (f32[64,512]{1,0:T(8,128)S(1)}, f32[8,128]{1,0:T(8,128)S(1)}) custom-call(f32[64,512]{1,0:T(8,128)S(1)} %bitcast.11, f32[64,512]{1,0:T(8,128)S(1)} %bitcast.12, f32[8,128]{1,0:T(8,128)S(1)} %bitcast.15, f32[8,3,128]{2,1,0:T(4,128)S(1)} %bitcast.14, s32[8,128]{1,0:T(8,128)S(1)} %bitcast.16, s32[8,128]{1,0:T(8,128)S(1)} %bitcast.17, s32[8]{0:T(128)S(1)} %bitcast.19), custom_call_target="tpu_custom_call" | custom-call | tf_op jit(solution)/shard_map/heat_step/pallas_call | solution.py:422
  73.5 0.7 copy.14
  74.2 0.6 copy.15
Async XLA Ops:
  0.6 0.8 %copy-start.2 = (f32[1,1,8,128]{3,2,1,0:T(8,128)S(1)}, f32[1,1,8,128]{3,2,1,0:T(8,128)}, u32[]{:S(2)}) copy-start(f32[1,1,8,128]{3,2,1,0:T(8,128)} %param.9) | copy-start | bytes 12292
  0.6 0.8 %copy-start.3 = (s32[1,1,8,128]{3,2,1,0:T(8,128)S(1)}, s32[1,1,8,128]{3,2,1,0:T(8,128)}, u32[]{:S(2)}) copy-start(s32[1,1,8,128]{3,2,1,0:T(8,128)} %param.11) | copy-start | bytes 12292
  0.7 0.8 %copy-start.4 = (s32[1,1,8,128]{3,2,1,0:T(8,128)S(1)}, s32[1,1,8,128]{3,2,1,0:T(8,128)}, u32[]{:S(2)}) copy-start(s32[1,1,8,128]{3,2,1,0:T(8,128)} %param.12) | copy-start | bytes 12292
  1.4 0.7 copy-start.5
  2.0 0.9 %copy-start = (f32[2,32,512]{2,1,0:T(8,128)S(1)}, f32[2,32,512]{2,1,0:T(8,128)}, u32[]{:S(2)}) copy-start(f32[2,32,512]{2,1,0:T(8,128)} %param.7) | copy-start | bytes 393220
  3.0 0.9 %copy-start.1 = (f32[2,32,512]{2,1,0:T(8,128)S(1)}, f32[2,32,512]{2,1,0:T(8,128)}, u32[]{:S(2)}) copy-start(f32[2,32,512]{2,1,0:T(8,128)} %param.8) | copy-start | bytes 393220

commit v2 on v1

--- a/solution.py
+++ b/solution.py
@@ -21,8 +21,8 @@
     nb,
     layers,
     chunk,
-    v_ref,
-    k_ref,
+    v_hbm,
+    k_hbm,
     joules_ref,
     local_ref,
     anchor_ref,
@@ -43,6 +43,8 @@
     weight_y,
     read_out,
     read_in,
+    v_ref,
+    k_ref,
     halo_send,
     halo_recv,
     sum_send,
@@ -51,6 +53,7 @@
     atom_recv,
     read_send,
     read_recv,
+    load_sem,
 ):
     s = lax.axis_index("slab")
     b = lax.axis_index("brick")
@@ -59,6 +62,11 @@
     slots = joules_ref.shape[1]
     devices = ns * nb
     me = s * nb + b
+
+    load_k = pltpu.make_async_copy(k_hbm, k_ref, load_sem.at[0])
+    load_v = pltpu.make_async_copy(v_hbm, v_ref, load_sem.at[1])
+    load_k.start()
+    load_v.start()
 
     def wrapped(index, count):
         return jnp.where(index >= count, index - count, index)
@@ -180,10 +188,13 @@
     for owner in range(ns):
         here = slice(owner, owner + 1)
         atoms_out[owner, 0:1, :] = heat[here]
-        atoms_out[owner, 1:4, :] = local_ref[owner]
+        for axis in range(3):
+            atoms_out[owner, axis + 1 : axis + 2, :] = local_ref[axis, here]
         atoms_out[owner, 4:5, :] = line[here]
         atoms_out[owner, 5:6, :] = column[here]
         atoms_out[owner, 6:8, :] = jnp.zeros((2, slots), jnp.float32)
+    load_k.wait()
+    load_v.wait()
     stage_faces(0, k_ref)
     stage_faces(1, v_ref)
     pl.semaphore_wait(barrier, devices - 1)
@@ -302,15 +313,30 @@
     wait_halo(2, fields.at[0])
     fields[1] = operator(residual, 2)
 
+    def interpolate(part, carry):
+        lifted = jnp.dot(
+            jnp.concatenate([x_ref[...], vectors[0], vectors[1]], axis=0),
+            weight_y[part],
+            precision=HIGHEST,
+            preferred_element_type=jnp.float32,
+        )
+        weights = weight_zx[part]
+        for kind in range(3):
+            read = jnp.sum(
+                lifted[kind * rows : (kind + 1) * rows] * weights, axis=0, keepdims=True
+            )
+            for index in range(chunk):
+                read_out[part * chunk + index, kind : kind + 1, :] = read[
+                    :, index * slots : (index + 1) * slots
+                ]
+        return carry
+
     before_rr = None
     before_alpha = None
     for step in range(ITERS):
         last = step == ITERS - 1
         image = fields.at[step + 1]
         turn = step + 3
-        if not last:
-            stage_faces(turn, image)
-            start_halo(turn, image)
         r = vectors[0]
         w = image[...]
         sums[step, me] = jnp.concatenate(
@@ -339,8 +365,18 @@
 
         for_peers(lambda ps, pb: sum_copy(sums.at[step, me], ps, pb).start())
         if not last:
+            stage_faces(turn, image)
+            start_halo(turn, image)
             wait_halo(turn, image)
             q = operator(w, turn)
+        else:
+            lax.fori_loop(0, ns // chunk, interpolate, 0)
+            for_slabs(
+                lambda peer: atom_copy(
+                    peer, read_out.at[peer], read_in.at[s], read_send, read_recv
+                ).start()
+            )
+            read_in[s] = read_out[s]
         sum_copy(
             sums.at[step, pl.ds(0, devices - 1)], wrapped(s + 1, ns), b
         ).wait()
@@ -369,24 +405,6 @@
             vectors[3] = zp
         before_rr, before_alpha = rr, alpha
 
-    x = x_ref[...]
-
-    def interpolate(part, carry):
-        lifted = jnp.dot(
-            x, weight_y[part], precision=HIGHEST, preferred_element_type=jnp.float32
-        )
-        read = jnp.sum(lifted * weight_zx[part], axis=0, keepdims=True)
-        for index in range(chunk):
-            read_out[part * chunk + index] = read[:, index * slots : (index + 1) * slots]
-        return carry
-
-    lax.fori_loop(0, ns // chunk, interpolate, 0)
-    for_slabs(
-        lambda peer: atom_copy(
-            peer, read_out.at[peer], read_in.at[s], read_send, read_recv
-        ).start()
-    )
-    read_in[s] = read_out[s]
     end_halo(0, k_ref)
     end_halo(1, v_ref)
     for turn in range(2, ROUNDS):
@@ -396,7 +414,10 @@
     ).wait()
     for owner in range(ns):
         probe_ref[owner : owner + 1, :] = jnp.where(
-            live[owner : owner + 1], read_in[owner], 0.0
+            live[owner : owner + 1],
+            read_in[owner, 0:1, :]
+            + alpha * (read_in[owner, 1:2, :] + beta * read_in[owner, 2:3, :]),
+            0.0,
         )
 
 
@@ -425,7 +446,9 @@
             jax.ShapeDtypeStruct((rows, columns), f32),
             jax.ShapeDtypeStruct((ns, slots), f32),
         ),
-        in_specs=[vmem] * 6 + [pl.BlockSpec(memory_space=pltpu.SMEM)],
+        in_specs=[pl.BlockSpec(memory_space=pl.ANY)] * 2
+        + [vmem] * 4
+        + [pl.BlockSpec(memory_space=pltpu.SMEM)],
         out_specs=(vmem, vmem),
         scratch_shapes=[
             pltpu.VMEM((7, rows, columns), f32),
@@ -439,8 +462,10 @@
             pltpu.VMEM((ns, 8, slots), f32),
             pltpu.VMEM((parts, rows, chunk * slots), f32),
             pltpu.VMEM((parts, columns, chunk * slots), f32),
-            pltpu.VMEM((ns, 1, slots), f32),
-            pltpu.VMEM((ns, 1, slots), f32),
+            pltpu.VMEM((ns, 3, slots), f32),
+            pltpu.VMEM((ns, 3, slots), f32),
+            pltpu.VMEM((rows, columns), f32),
+            pltpu.VMEM((rows, columns), f32),
             dma((ROUNDS, 4)),
             dma((ROUNDS, 4)),
             dma((ITERS,)),
@@ -449,6 +474,7 @@
             dma,
             dma,
             dma,
+            dma((2,)),
         ],
         compiler_params=pltpu.CompilerParams(
             collective_id=0, has_side_effects=True, vmem_limit_bytes=48 * 1024 * 1024
@@ -458,7 +484,7 @@
         opening_warmth_values.reshape(rows, columns),
         thermal_diffusivity_field.reshape(rows, columns),
         atom_released_joules.reshape(ns, slots),
-        atom_local_coordinates.reshape(ns, 3, slots),
+        jnp.swapaxes(atom_local_coordinates.reshape(ns, 3, slots), 0, 1),
         atom_anchor_voxel.reshape(ns, slots),
         atom_oxygen_flag.reshape(ns, slots),
         live_entries_number.reshape(ns),

time: 75 us -> 68.2 us (0.909)
  Pallas kernels: 69.7 us -> 61.4 us
  local copies, waits for them, and re-layouts: 4.43 us -> 5.81 us
    pallas_call x1, Pallas kernels: 69.7 us -> 61.4 us  [per_device(): pl.pallas_call(functools.partial(step_kernel, ns, nb, layers, chunk), out...]
    unnamed x15 -> x16, local copies, waits for them, and re-layouts: 4.43 us -> 5.81 us
where the time goes in v2:
time: 68.2 us; the launch traced here: 67.8 us
  Pallas kernels  61.4 us (90%)
  local copies, waits for them, and re-layouts  5.81 us (9%)
    pallas_call x1, Pallas kernels, per_device(): pl.pallas_call(functools.partial(step_kernel, ns, nb, layers, chunk), out...  61.4 us
    unnamed x16, local copies, waits for them, and re-layouts  5.81 us

profile of v2, /device:TPU:0, one launch (start us, length us, event | category | flops | bytes accessed | tf_op | source)
XLA Modules:
  0.0 67.8 jit_solution(451157884413112000)
XLA Ops:
  0.6 0.0 copy-start.2
  0.6 0.0 copy-start.6
  0.7 0.7 %copy-done.2 = f32[1,1,8,3,128]{4,2,3,1,0:T(8,128)S(1)} copy-done((f32[1,1,8,3,128]{4,2,3,1,0:T(8,128)S(1)}, f32[1,1,8,3,128]{4,2,3,1,0:T(8,128)}, u32[]{:S(2)}) %copy-start.2) | copy-done | bytes 12312
  1.3 0.0 copy-done.6
  1.3 0.0 copy-start
  1.3 0.9 %copy-done = f32[2,32,512]{2,1,0:T(8,128)S(1)} copy-done((f32[2,32,512]{2,1,0:T(8,128)S(1)}, f32[2,32,512]{2,1,0:T(8,128)}, u32[]{:S(2)}) %copy-start) | copy-done | bytes 131096
  2.2 0.0 copy-start.1
  2.2 0.9 %copy-done.1 = f32[2,32,512]{2,1,0:T(8,128)S(1)} copy-done((f32[2,32,512]{2,1,0:T(8,128)S(1)}, f32[2,32,512]{2,1,0:T(8,128)}, u32[]{:S(2)}) %copy-start.1) | copy-done | bytes 131096
  3.2 0.0 copy-start.3
  3.2 0.7 %copy-done.3 = f32[1,1,8,128]{3,2,1,0:T(8,128)S(1)} copy-done((f32[1,1,8,128]{3,2,1,0:T(8,128)S(1)}, f32[1,1,8,128]{3,2,1,0:T(8,128)}, u32[]{:S(2)}) %copy-start.3) | copy-done | bytes 4120
  3.8 0.0 copy-start.4
  3.8 0.7 %copy-done.4 = s32[1,1,8,128]{3,2,1,0:T(8,128)S(1)} copy-done((s32[1,1,8,128]{3,2,1,0:T(8,128)S(1)}, s32[1,1,8,128]{3,2,1,0:T(8,128)}, u32[]{:S(2)}) %copy-start.4) | copy-done | bytes 4120
  4.5 0.0 copy-start.5
  4.5 0.7 %copy-done.5 = s32[1,1,8,128]{3,2,1,0:T(8,128)S(1)} copy-done((s32[1,1,8,128]{3,2,1,0:T(8,128)S(1)}, s32[1,1,8,128]{3,2,1,0:T(8,128)}, u32[]{:S(2)}) %copy-start.5) | copy-done | bytes 4120
  5.2 61.4 %heat_step.1 = (f32[64,512]{1,0:T(8,128)S(1)}, f32[8,128]{1,0:T(8,128)S(1)}) custom-call(f32[64,512]{1,0:T(8,128)S(1)} %bitcast.11, f32[64,512]{1,0:T(8,128)S(1)} %bitcast.12, f32[8,128]{1,0:T(8,128)S(1)} %bitcast.15, f32[3,8,128]{2,1,0:T(8,128)S(1)} %bitcast.14, s32[8,128]{1,0:T(8,128)S(1)} %bitcast.16, s32[8,128]{1,0:T(8,128)S(1)} %bitcast.17, s32[8]{0:T(128)S(1)} %bitcast.19), custom_call_target="tpu_custom_call" | custom-call | tf_op jit(solution)/shard_map/heat_step/pallas_call | solution.py:443
  66.6 0.7 copy.11
  67.2 0.6 copy.12
Async XLA Ops:
  0.6 0.7 %copy-start.2 = (f32[1,1,8,3,128]{4,2,3,1,0:T(8,128)S(1)}, f32[1,1,8,3,128]{4,2,3,1,0:T(8,128)}, u32[]{:S(2)}) copy-start(f32[1,1,8,3,128]{4,2,3,1,0:T(8,128)} %param.10) | copy-start | bytes 36868
  0.6 0.7 %copy-start.6 = (s32[1,1,8]{2,1,0:T(1,128)S(1)}, s32[1,1,8]{2,1,0:T(1,128)}, u32[]{:S(2)}) copy-start(s32[1,1,8]{2,1,0:T(1,128)} %param.13) | copy-start | bytes 100
  1.3 0.9 %copy-start = (f32[2,32,512]{2,1,0:T(8,128)S(1)}, f32[2,32,512]{2,1,0:T(8,128)}, u32[]{:S(2)}) copy-start(f32[2,32,512]{2,1,0:T(8,128)} %param.7) | copy-start | bytes 393220
  2.2 0.9 %copy-start.1 = (f32[2,32,512]{2,1,0:T(8,128)S(1)}, f32[2,32,512]{2,1,0:T(8,128)}, u32[]{:S(2)}) copy-start(f32[2,32,512]{2,1,0:T(8,128)} %param.8) | copy-start | bytes 393220
  3.2 0.7 %copy-start.3 = (f32[1,1,8,128]{3,2,1,0:T(8,128)S(1)}, f32[1,1,8,128]{3,2,1,0:T(8,128)}, u32[]{:S(2)}) copy-start(f32[1,1,8,128]{3,2,1,0:T(8,128)} %param.9) | copy-start | bytes 12292
  3.8 0.7 %copy-start.4 = (s32[1,1,8,128]{3,2,1,0:T(8,128)S(1)}, s32[1,1,8,128]{3,2,1,0:T(8,128)}, u32[]{:S(2)}) copy-start(s32[1,1,8,128]{3,2,1,0:T(8,128)} %param.11) | copy-start | bytes 12292
  4.5 0.7 %copy-start.5 = (s32[1,1,8,128]{3,2,1,0:T(8,128)S(1)}, s32[1,1,8,128]{3,2,1,0:T(8,128)}, u32[]{:S(2)}) copy-start(s32[1,1,8,128]{3,2,1,0:T(8,128)} %param.12) | copy-start | bytes 12292

commit v3 on v2

--- a/solution.py
+++ b/solution.py
@@ -331,6 +331,7 @@
                 ]
         return carry
 
+    left_half = lax.broadcasted_iota(jnp.int32, (1, 128), 1) < 64
     before_rr = None
     before_alpha = None
     for step in range(ITERS):
@@ -339,18 +340,20 @@
         turn = step + 3
         r = vectors[0]
         w = image[...]
-        sums[step, me] = jnp.concatenate(
-            [
+        narrow = [
+            jnp.sum(
                 functools.reduce(
-                    jnp.add,
-                    [
-                        jnp.sum(item, axis=0, keepdims=True)[:, at : at + 128]
-                        for at in range(0, columns, 128)
-                    ],
-                )
-                for item in (r * r, r * w)
-            ],
+                    jnp.add, [item[:, at : at + 128] for at in range(0, columns, 128)]
+                ).reshape(rows // 8, 8, 128),
+                axis=0,
+            )
+            for item in (r * r, r * w)
+        ]
+        sums[step, me] = jnp.sum(
+            jnp.where(left_half, narrow[0], narrow[1])
+            + pltpu.roll(jnp.where(left_half, narrow[1], narrow[0]), 64, 1),
             axis=0,
+            keepdims=True,
         )
 
         def sum_copy(part, ps, pb):
@@ -364,6 +367,8 @@
             )
 
         for_peers(lambda ps, pb: sum_copy(sums.at[step, me], ps, pb).start())
+        if step > 0:
+            x_ref[...] = x_ref[...] + before_alpha * vectors[1]
         if not last:
             stage_faces(turn, image)
             start_halo(turn, image)
@@ -380,10 +385,9 @@
         sum_copy(
             sums.at[step, pl.ds(0, devices - 1)], wrapped(s + 1, ns), b
         ).wait()
-        total = jnp.sum(
-            jnp.sum(sums[step], axis=0), axis=1, keepdims=True
-        )
-        rr, rw = total[0:1], total[1:2]
+        total = jnp.sum(sums[step], axis=0)
+        rr = jnp.sum(jnp.where(left_half, total, 0.0), axis=1, keepdims=True)
+        rw = jnp.sum(jnp.where(left_half, 0.0, total), axis=1, keepdims=True)
         if step == 0:
             alpha = rr / rw
             p = r
@@ -396,8 +400,9 @@
             if not last:
                 sp = w + beta * vectors[2]
                 zp = q + beta * vectors[3]
-        x_ref[...] = x_ref[...] + alpha * p
-        if not last:
+        if last:
+            x_ref[...] = x_ref[...] + alpha * p
+        else:
             vectors[0] = r - alpha * sp
             fields[step + 2] = w - alpha * zp
             vectors[1] = p
@@ -457,7 +462,7 @@
             pltpu.VMEM((ROUNDS, 2, lines, columns), f32),
             pltpu.VMEM((ROUNDS, 2, layers, columns), f32),
             pltpu.VMEM((ROUNDS, 2, layers, columns), f32),
-            pltpu.VMEM((ITERS, ns * nb, 2, 128), f32),
+            pltpu.VMEM((ITERS, ns * nb, 1, 128), f32),
             pltpu.VMEM((ns, 8, slots), f32),
             pltpu.VMEM((ns, 8, slots), f32),
             pltpu.VMEM((parts, rows, chunk * slots), f32),

time: 68.2 us -> 66.5 us (0.975)
  Pallas kernels: 61.4 us -> 59.7 us
    pallas_call x1, Pallas kernels: 61.4 us -> 59.7 us  [per_device(): pl.pallas_call(functools.partial(step_kernel, ns, nb, layers, chunk), out...]
where the time goes in v3:
time: 66.5 us; the launch traced here: 66.2 us
  Pallas kernels  59.7 us (90%)
  local copies, waits for them, and re-layouts  5.81 us (9%)
    pallas_call x1, Pallas kernels, per_device(): pl.pallas_call(functools.partial(step_kernel, ns, nb, layers, chunk), out...  59.7 us
    unnamed x16, local copies, waits for them, and re-layouts  5.81 us

profile of v3, /device:TPU:0, one launch (start us, length us, event | category | flops | bytes accessed | tf_op | source)
XLA Modules:
  0.0 66.2 jit_solution(15137662328802307552)
XLA Ops:
  0.6 0.0 copy-start.2
  0.6 0.0 copy-start.6
  0.7 0.7 %copy-done.2 = f32[1,1,8,3,128]{4,2,3,1,0:T(8,128)S(1)} copy-done((f32[1,1,8,3,128]{4,2,3,1,0:T(8,128)S(1)}, f32[1,1,8,3,128]{4,2,3,1,0:T(8,128)}, u32[]{:S(2)}) %copy-start.2) | copy-done | bytes 12312
  1.3 0.0 copy-done.6
  1.3 0.0 copy-start
  1.3 0.9 %copy-done = f32[2,32,512]{2,1,0:T(8,128)S(1)} copy-done((f32[2,32,512]{2,1,0:T(8,128)S(1)}, f32[2,32,512]{2,1,0:T(8,128)}, u32[]{:S(2)}) %copy-start) | copy-done | bytes 131096
  2.2 0.0 copy-start.1
  2.2 0.9 %copy-done.1 = f32[2,32,512]{2,1,0:T(8,128)S(1)} copy-done((f32[2,32,512]{2,1,0:T(8,128)S(1)}, f32[2,32,512]{2,1,0:T(8,128)}, u32[]{:S(2)}) %copy-start.1) | copy-done | bytes 131096
  3.2 0.0 copy-start.3
  3.2 0.7 %copy-done.3 = f32[1,1,8,128]{3,2,1,0:T(8,128)S(1)} copy-done((f32[1,1,8,128]{3,2,1,0:T(8,128)S(1)}, f32[1,1,8,128]{3,2,1,0:T(8,128)}, u32[]{:S(2)}) %copy-start.3) | copy-done | bytes 4120
  3.8 0.0 copy-start.4
  3.8 0.7 %copy-done.4 = s32[1,1,8,128]{3,2,1,0:T(8,128)S(1)} copy-done((s32[1,1,8,128]{3,2,1,0:T(8,128)S(1)}, s32[1,1,8,128]{3,2,1,0:T(8,128)}, u32[]{:S(2)}) %copy-start.4) | copy-done | bytes 4120
  4.5 0.0 copy-start.5
  4.5 0.7 %copy-done.5 = s32[1,1,8,128]{3,2,1,0:T(8,128)S(1)} copy-done((s32[1,1,8,128]{3,2,1,0:T(8,128)S(1)}, s32[1,1,8,128]{3,2,1,0:T(8,128)}, u32[]{:S(2)}) %copy-start.5) | copy-done | bytes 4120
  5.2 59.7 %heat_step.1 = (f32[64,512]{1,0:T(8,128)S(1)}, f32[8,128]{1,0:T(8,128)S(1)}) custom-call(f32[64,512]{1,0:T(8,128)S(1)} %bitcast.11, f32[64,512]{1,0:T(8,128)S(1)} %bitcast.12, f32[8,128]{1,0:T(8,128)S(1)} %bitcast.15, f32[3,8,128]{2,1,0:T(8,128)S(1)} %bitcast.14, s32[8,128]{1,0:T(8,128)S(1)} %bitcast.16, s32[8,128]{1,0:T(8,128)S(1)} %bitcast.17, s32[8]{0:T(128)S(1)} %bitcast.19), custom_call_target="tpu_custom_call" | custom-call | tf_op jit(solution)/shard_map/heat_step/pallas_call | solution.py:448
  64.9 0.7 copy.11
  65.6 0.6 copy.12
Async XLA Ops:
  0.6 0.7 %copy-start.2 = (f32[1,1,8,3,128]{4,2,3,1,0:T(8,128)S(1)}, f32[1,1,8,3,128]{4,2,3,1,0:T(8,128)}, u32[]{:S(2)}) copy-start(f32[1,1,8,3,128]{4,2,3,1,0:T(8,128)} %param.10) | copy-start | bytes 36868
  0.6 0.7 %copy-start.6 = (s32[1,1,8]{2,1,0:T(1,128)S(1)}, s32[1,1,8]{2,1,0:T(1,128)}, u32[]{:S(2)}) copy-start(s32[1,1,8]{2,1,0:T(1,128)} %param.13) | copy-start | bytes 100
  1.3 0.9 %copy-start = (f32[2,32,512]{2,1,0:T(8,128)S(1)}, f32[2,32,512]{2,1,0:T(8,128)}, u32[]{:S(2)}) copy-start(f32[2,32,512]{2,1,0:T(8,128)} %param.7) | copy-start | bytes 393220
  2.2 0.9 %copy-start.1 = (f32[2,32,512]{2,1,0:T(8,128)S(1)}, f32[2,32,512]{2,1,0:T(8,128)}, u32[]{:S(2)}) copy-start(f32[2,32,512]{2,1,0:T(8,128)} %param.8) | copy-start | bytes 393220
  3.2 0.7 %copy-start.3 = (f32[1,1,8,128]{3,2,1,0:T(8,128)S(1)}, f32[1,1,8,128]{3,2,1,0:T(8,128)}, u32[]{:S(2)}) copy-start(f32[1,1,8,128]{3,2,1,0:T(8,128)} %param.9) | copy-start | bytes 12292
  3.8 0.7 %copy-start.4 = (s32[1,1,8,128]{3,2,1,0:T(8,128)S(1)}, s32[1,1,8,128]{3,2,1,0:T(8,128)}, u32[]{:S(2)}) copy-start(s32[1,1,8,128]{3,2,1,0:T(8,128)} %param.11) | copy-start | bytes 12292
  4.5 0.7 %copy-start.5 = (s32[1,1,8,128]{3,2,1,0:T(8,128)S(1)}, s32[1,1,8,128]{3,2,1,0:T(8,128)}, u32[]{:S(2)}) copy-start(s32[1,1,8,128]{3,2,1,0:T(8,128)} %param.12) | copy-start | bytes 12292
